TPU v7x, 32 devices: a whole 2x2x4 slice. The times are simulated.
32 devices in a mesh: dp: 4 (over z), table: 8 (over y, x, core).
Axes of the slice: x: 2, y: 2, z: 4, core: 2. Of those that a mesh axis runs over, the one named last changes fastest.
Arguments:
- queries: bfloat16 [4096, 2, 512], P(('dp', 'table')), may hold values from -6 to 6
- sub_keys: bfloat16 [2, 2, 512, 256], replicated, may hold values from -0.375 to 0.375
- values: bfloat16 [512, 512, 1024], P('table', None, 'dp'), may hold values from -0.1875 to 0.1875
- slot_first: int32 [4096, 2, 4], P(('dp', 'table')), may hold values from 0 to 511, as said below
- slot_second: int32 [4096, 2, 4], P(('dp', 'table')), may hold values from 0 to 511
- cotangent: bfloat16 [4096, 1024], P(('dp', 'table')), may hold values from -6 to 6
Outputs:
- value_update: float32 [512, 512, 1024], P('table', None, 'dp')
- key_update: float32 [2, 2, 512, 256], P(None, None, ('dp', 'table'))
- clip_factor: float32 [1], replicated
Inputs may be any that keep to these rules, and one draw needn't show every extreme that they name: Within each aligned block of 128 tokens (the tokens of one device), at most 192 of its 1024 slots have slot_first in any one range [r * 64, (r + 1) * 64), and exactly 192 do in one such range.
All inputs are finite; a program needn't handle non-finite values.
Results may differ from a plain program's by a relative error of at most 0.0003.
Values may be sent and summed in bfloat16 or wider, within the bound.
A program may use at most 128 MiB of HBM per device.

v0:
```python
import math

import jax
import jax.numpy as jnp
from jax import lax
from jax.sharding import PartitionSpec as P

limit_ratio = 5.0


def key_terms(dscore, query_half, key_index, key_count):
    labels = jnp.arange(key_count, dtype=jnp.int32)
    weighted = jnp.sum(
        jnp.where(key_index[:, :, :, None] == labels, dscore[:, :, :, None], 0.0), axis=2
    )
    return jnp.einsum(
        "thi,thc->hic", weighted, query_half.astype(jnp.float32), precision=lax.Precision.HIGHEST
    )


def local(queries, sub_keys, values, slot_first, slot_second, cotangent):
    table_size = lax.axis_size("table")
    data_size = lax.axis_size("dp")
    token_count = slot_first.shape[0]
    head_count = slot_first.shape[1]
    pick_count = slot_first.shape[2]
    half_width = queries.shape[2] // 2
    key_count = sub_keys.shape[2]
    first_block = values.shape[0]
    column_count = values.shape[2]
    slot_count = token_count * head_count * pick_count
    capacity = 3 * slot_count // (2 * table_size)
    head_ids = jnp.arange(head_count, dtype=jnp.int32)[None, :, None]
    query_first = queries[:, :, :half_width]
    query_second = queries[:, :, half_width:]
    key_first = sub_keys[0][head_ids, slot_first]
    key_second = sub_keys[1][head_ids, slot_second]
    raw_score = jnp.einsum(
        "thc,thkc->thk", query_first, key_first, preferred_element_type=jnp.float32
    )
    raw_score = raw_score + jnp.einsum(
        "thc,thkc->thk", query_second, key_second, preferred_element_type=jnp.float32
    )
    exp_score = jnp.exp(raw_score)
    weight = exp_score / jnp.sum(exp_score, axis=2, keepdims=True)
    owner_group = (slot_first // first_block).reshape(slot_count)
    local_row = (slot_first % first_block * key_count + slot_second).reshape(slot_count)
    token_row = jnp.broadcast_to(
        jnp.arange(token_count, dtype=jnp.int32)[:, None, None], slot_first.shape
    ).reshape(slot_count)
    member = (owner_group[:, None] == jnp.arange(table_size, dtype=jnp.int32)[None, :]).astype(
        jnp.int32
    )
    before = jnp.sum((jnp.cumsum(member, axis=0) - member) * member, axis=1)
    target = owner_group * capacity + before
    send_rows = (
        jnp.zeros((table_size * capacity,), jnp.int32)
        .at[target]
        .set(local_row)
        .reshape(table_size, capacity)
    )
    send_weight = (
        jnp.zeros((table_size * capacity,), jnp.float32)
        .at[target]
        .set(weight.reshape(slot_count))
        .reshape(table_size, capacity)
    )
    send_token = (
        jnp.zeros((table_size * capacity,), jnp.int32)
        .at[target]
        .set(token_row)
        .reshape(table_size, capacity)
    )
    cot_columns = lax.all_to_all(cotangent, "dp", split_axis=1, concat_axis=0, tiled=True)
    cot_all = lax.all_gather(cot_columns, "table", axis=0, tiled=True)
    received = (
        lax.all_to_all(send_rows, "table", split_axis=0, concat_axis=0, tiled=True),
        lax.all_to_all(send_weight, "table", split_axis=0, concat_axis=0, tiled=True),
        lax.all_to_all(send_token, "table", split_axis=0, concat_axis=0, tiled=True),
    )
    rows_all, weight_all, token_all = (
        lax.all_gather(received[0], "dp", axis=0, tiled=True),
        lax.all_gather(received[1], "dp", axis=0, tiled=True),
        lax.all_gather(received[2], "dp", axis=0, tiled=True),
    )
    source_index = jnp.arange(data_size * table_size, dtype=jnp.int32)[:, None]
    position = (
        source_index % table_size * data_size + source_index // table_size
    ) * token_count + token_all
    table_flat = values.reshape(first_block * key_count, column_count)
    rows_flat = rows_all.reshape(-1)
    weight_flat = weight_all.reshape(-1)
    cot_part = cot_all[position.reshape(-1)]
    value_part = table_flat[rows_flat]
    partial_dots = jnp.einsum("rc,rc->r", cot_part, value_part, preferred_element_type=jnp.float32)
    start = jnp.zeros((first_block * key_count, column_count), jnp.float32)
    value_grad = start.at[rows_flat].add(weight_flat[:, None] * cot_part.astype(jnp.float32))
    partial_dots = partial_dots.reshape(data_size, table_size, capacity)
    own_share = lax.psum_scatter(partial_dots, "dp", scatter_dimension=0, tiled=True)[0]
    returned = lax.all_to_all(own_share, "table", split_axis=0, concat_axis=0, tiled=True)
    picked = returned.reshape(table_size * capacity)[target].reshape(
        token_count, head_count, pick_count
    )
    dscore = weight * (picked - jnp.sum(weight * picked, axis=2, keepdims=True))
    key_grad = jnp.stack(
        [
            key_terms(dscore, query_first, slot_first, key_count),
            key_terms(dscore, query_second, slot_second, key_count),
        ]
    )
    value_sq = jnp.sum(value_grad * value_grad)
    share_rows = key_count // (data_size * table_size)
    key_full = lax.psum(key_grad, ("dp", "table"))
    key_part = lax.dynamic_slice_in_dim(
        key_full, lax.axis_index(("dp", "table")) * share_rows, share_rows, 2
    )
    added_sq = jnp.sum(key_full * key_full)
    total_sq = lax.psum(value_sq, ("dp", "table")) + added_sq
    all_tokens = token_count * data_size * table_size
    clip_factor = jnp.minimum(1.0, limit_ratio * math.sqrt(all_tokens) / jnp.sqrt(total_sq))
    value_update = (clip_factor * value_grad).reshape(first_block, key_count, column_count)
    key_update = clip_factor * key_part
    return (value_update, key_update, clip_factor.reshape(1))


def solution(mesh):
    placed = (
        P(("dp", "table"), None, None),
        P(),
        P("table", None, "dp"),
        P(("dp", "table"), None, None),
        P(("dp", "table"), None, None),
        P(("dp", "table"), None),
    )
    return jax.shard_map(
        local,
        mesh=mesh,
        in_specs=placed,
        out_specs=(P("table", None, "dp"), P(None, None, ("dp", "table"), None), P()),
        check_vma=False,
    )
```

profile of v0, /device:TPU:0, one launch (start us, length us, event | category | flops | bytes accessed | tf_op | source)
XLA Modules:
  0.0 374.1 jit_solution(15670014093752232717)
XLA Ops:
  8.8 6.3 %all-to-all-start.2 = ((bf16[128,4,256]{2,0,1:T(8,128)(2,1)}), bf16[128,4,256]{2,0,1:T(8,128)(2,1)S(1)}, u32[]{:S(2)}, u32[]{:S(2)}) async-start(bf16[128,4,256]{2,0,1:T(8,128)(2,1)} %bitcast.66), calls=%async_computation.2 | async-start | bytes 524288 | tf_op jit(solution)/shard_map/all_to_all | solution.py:74
  20.7 4.3 %scatter_custom_fusion = s32[1536]{0:T(1024)S(1)} fusion(s32[1024]{0:T(1024)S(1)} %bitcast.76, s32[1024]{0:T(1024)S(1)} %reshape.278, s32[]{:T(128)} %constant.81.clone.1), kind=kCustom, calls=%fused_computation.80 | custom fusion | bytes 6148 | tf_op jit(solution)/shard_map/scatter | solution.py:59
  27.3 5.8 %gather_fusion = bf16[1024,256]{1,0:T(8,128)(2,1)S(1)} fusion(bf16[2,512,256]{2,1,0:T(8,128)(2,1)S(1)} %get-tuple-element.8, s32[1024]{0:T(1024)S(1)} %reshape.238), kind=kCustom, calls=%fused_computation | custom fusion | bytes 1056768 | tf_op jit(solution)/shard_map/gather | solution.py:36
  34.6 3.7 all-to-all-start
  39.3 4.3 %scatter_custom_fusion.2 = s32[1536]{0:T(1024)S(1)} fusion(s32[1024]{0:T(1024)S(1)} %bitcast.77, s32[1024]{0:T(1024)S(1)} %reshape.294, s32[]{:T(128)} %constant.81.clone.1), kind=kCustom, calls=%fused_computation.78 | custom fusion | bytes 6148 | tf_op jit(solution)/shard_map/scatter | solution.py:71
  44.7 5.8 %gather_fusion.1 = bf16[1024,256]{1,0:T(8,128)(2,1)S(1)} fusion(bf16[2,512,256]{2,1,0:T(8,128)(2,1)S(1)} %get-tuple-element.7, s32[1024]{0:T(1024)S(1)} %reshape.244), kind=kCustom, calls=%fused_computation.1 | custom fusion | bytes 1056768 | tf_op jit(solution)/shard_map/gather | solution.py:37
  51.4 4.2 %all-to-all-start.3 = ((s32[8,1,192]{2,1,0:T(1,128)}), s32[8,1,192]{2,1,0:T(1,128)S(1)}, u32[]{:S(2)}, u32[]{:S(2)}) async-start(s32[8,1,192]{2,1,0:T(1,128)} %all_to_all.54), calls=%async_computation.3 | async-start | bytes 16384 | tf_op jit(solution)/shard_map/all_to_all | solution.py:79
  55.7 13.7 %all-gather = s32[32,1,192]{2,1,0:T(1,128)S(1)} all-gather(s32[8,1,192]{2,1,0:T(1,128)S(1)} %all-to-all-done), channel_id=2, replica_groups=mesh['dp'=4,'table'=8] {'dp'}, dimensions={0}, use_global_device_ids=true | all-gather | bytes 30720 | tf_op jit(solution)/shard_map/all_gather | solution.py:82
  69.5 13.1 %all-gather.2 = s32[32,1,192]{2,1,0:T(1,128)S(1)} all-gather(s32[8,1,192]{2,1,0:T(1,128)S(1)} %all-to-all-done.3), channel_id=4, replica_groups=mesh['dp'=4,'table'=8] {'dp'}, dimensions={0}, use_global_device_ids=true | all-gather | bytes 30720 | tf_op jit(solution)/shard_map/all_gather | solution.py:84
  82.9 31.5 %gather_fusion.3 = bf16[6144,256]{1,0:T(8,128)(2,1)} fusion(bf16[32768,256]{1,0:T(8,128)(2,1)} %bitcast.68, s32[6144]{0:T(1024)S(1)} %broadcast_clamp_fusion), kind=kCustom, calls=%fused_computation.3 | custom fusion | bytes 6316032 | tf_op jit(solution)/shard_map/gather | solution.py:94
  115.0 24.1 %gather_fusion.2 = bf16[6144,256]{1,0:T(8,128)(2,1)S(1)} fusion(bf16[4096,256]{1,0:T(8,128)(2,1)} %all-gather.5.cloned.1.call-done, s32[6144]{0:T(1024)} %broadcast_clamp_fusion.1), kind=kCustom, calls=%fused_computation.2 | custom fusion | bytes 6316032 | tf_op jit(solution)/shard_map/gather | solution.py:93
  139.1 3.4 fusion.2
  146.1 18.3 %reduce-scatter.2.cloned.1.call-done = f32[1,8,192]{2,1,0:T(8,128)} async-done(((f32[4,8,192]{2,1,0:T(8,128)}), f32[1,8,192]{2,1,0:T(8,128)}) %reduce-scatter.2.cloned.1.call-update) | async-done | bytes 6160 | tf_op jit(solution)/shard_map/reduce_scatter | solution.py:99
  165.7 3.7 all-to-all-start.4
  169.4 4.7 %all-to-all-done.4 = f32[8,1,192]{2,1,0:T(1,128)S(1)} async-done(((f32[8,1,192]{2,1,0:T(1,128)}), f32[8,1,192]{2,1,0:T(1,128)S(1)}, u32[]{:S(2)}, u32[]{:S(2)}) %all-to-all-start.4) | async-done | bytes 6176 | tf_op jit(solution)/shard_map/all_to_all | solution.py:100
  174.2 10.5 %gather_fusion.4 = f32[1024]{0:T(1024)} fusion(f32[1536]{0:T(1024)S(1)} %reshape.234, s32[1024]{0:T(1024)S(1)} %broadcast_clamp_fusion.2), kind=kCustom, calls=%fused_computation.4 | custom fusion | bytes 12288 | tf_op jit(solution)/shard_map/gather | solution.py:101
  189.9 4.5 %scatter_custom_fusion.1 = f32[1536]{0:T(1024)S(1)} fusion(s32[1024]{0:T(1024)} %bitcast.79, f32[1024]{0:T(1024)} %reshape.286, f32[]{:T(128)} %constant.80.clone.1), kind=kCustom, calls=%fused_computation.75 | custom fusion | bytes 6656 | tf_op jit(solution)/shard_map/scatter | solution.py:65
  195.0 4.0 %all-to-all-start.1 = ((f32[8,1,192]{2,1,0:T(1,128)}), f32[8,1,192]{2,1,0:T(1,128)}, u32[]{:S(2)}, u32[]{:S(2)}) async-start(f32[8,1,192]{2,1,0:T(1,128)} %all_to_all.47), calls=%async_computation.1 | async-start | bytes 16384 | tf_op jit(solution)/shard_map/all_to_all | solution.py:78
  205.2 13.4 %all-gather.1 = f32[32,1,192]{2,1,0:T(1,128)S(1)} all-gather(f32[8,1,192]{2,1,0:T(1,128)} %all-to-all-done.1), channel_id=3, replica_groups=mesh['dp'=4,'table'=8] {'dp'}, dimensions={0}, use_global_device_ids=true | all-gather | bytes 30720 | tf_op jit(solution)/shard_map/all_gather | solution.py:83
  218.7 53.2 %scatter_custom_fusion.3 = f32[32768,256]{1,0:T(8,128)} fusion(s32[6144]{0:T(1024)} %bitcast.73, f32[]{:T(128)} %constant.80.clone.1, bf16[6144,256]{1,0:T(8,128)(2,1)S(1)} %gather_fusion.2, f32[6144]{0:T(1024)S(1)} %mul.89), kind=kCustom, calls=%fused_computation.11 | custom fusion | flops 4718592 | bytes 36725248 | tf_op jit(solution)/shard_map/scatter-add | solution.py:97
  272.0 15.6 %multiply_reduce_fusion = f32[]{:T(128)} fusion(f32[32768,256]{1,0:T(8,128)} %scatter_custom_fusion.3), kind=kLoop, calls=%fused_computation.9 | loop fusion | flops 16777215 | bytes 33554436 | tf_op jit(solution)/shard_map/reduce_sum | solution.py:111
  287.6 39.2 %psum.14 = f32[]{:T(128)} all-reduce(f32[]{:T(128)} %multiply_reduce_fusion), channel_id=1, replica_groups=mesh['dp'=4,'table'=8] {'dp','table'}, use_global_device_ids=true, to_apply=%region_9.10 | all-reduce | flops 1 | bytes 8 | tf_op jit(solution)/shard_map/psum | solution.py:118
  326.8 11.6 %all-reduce.2.cloned.1.call-done = f32[2,2,512,256]{3,2,1,0:T(8,128)} async-done(((f32[2,2,512,256]{3,2,1,0:T(8,128)}), f32[2,2,512,256]{3,2,1,0:T(8,128)}) %all-reduce.2.cloned.1.call-update) | async-done | bytes 2097168 | tf_op jit(solution)/shard_map/psum | solution.py:113
  342.5 22.5 %broadcast_multiply_fusion = f32[32768,256]{1,0:T(8,128)} fusion(f32[32768,256]{1,0:T(8,128)} %scatter_custom_fusion.3, f32[]{:T(128)} %min_shard_map.3), kind=kLoop, calls=%fused_computation.10 | loop fusion | flops 8388608 | bytes 67108864 | tf_op jit(solution)/shard_map/mul | solution.py:121
  (84 shorter events, 36.1 us)
Async XLA Ops:
  8.8 25.8 %all-to-all-start.2 = ((bf16[128,4,256]{2,0,1:T(8,128)(2,1)}), bf16[128,4,256]{2,0,1:T(8,128)(2,1)S(1)}, u32[]{:S(2)}, u32[]{:S(2)}) async-start(bf16[128,4,256]{2,0,1:T(8,128)(2,1)} %bitcast.66), calls=%async_computation.2 | async-start | bytes 524288 | tf_op jit(solution)/shard_map/all_to_all | solution.py:74
  20.7 148.7 %copy-start.5 = (s32[1024,1]{0,1:T(1,128)}, s32[1024,1]{0,1:T(1,128)S(1)}, u32[]{:S(2)}) copy-start(s32[1024,1]{0,1:T(1,128)S(1)} %compare_select_fusion.2) | copy-start | bytes 12292
  27.3 6.0 %copy-start.1 = (bf16[128,2,512]{2,1,0:T(2,128)(2,1)S(1)}, bf16[128,2,512]{2,1,0:T(2,128)(2,1)}, u32[]{:S(2)}) copy-start(bf16[128,2,512]{2,1,0:T(2,128)(2,1)} %param.6) | copy-start | bytes 786436
  33.1 5.9 %copy-start.4 = (s32[128,2,4]{0,2,1:T(4,128)S(1)}, s32[128,2,4]{0,2,1:T(4,128)}, u32[]{:S(2)}) copy-start(s32[128,2,4]{0,2,1:T(4,128)} %param.10) | copy-start | bytes 12292
  34.6 3.8 %copy-start = (bf16[128,4,256]{2,0,1:T(8,128)(2,1)}, bf16[128,4,256]{2,0,1:T(8,128)(2,1)S(1)}, u32[]{:S(2)}) copy-start(bf16[128,4,256]{2,0,1:T(8,128)(2,1)S(1)} %all-to-all-done.2) | copy-start | bytes 786436
  34.6 16.8 %all-to-all-start = ((s32[8,1,192]{2,1,0:T(1,128)}), s32[8,1,192]{2,1,0:T(1,128)S(1)}, u32[]{:S(2)}, u32[]{:S(2)}) async-start(s32[8,1,192]{2,1,0:T(1,128)} %all_to_all.44), calls=%async_computation | async-start | bytes 16384 | tf_op jit(solution)/shard_map/all_to_all | solution.py:77
  38.3 76.7 %all-gather.5.cloned.1.call-start = ((), (), s32[]{:S(2)}) async-start(), calls=%async_computation.6 | async-start | bytes 2359296 | tf_op jit(solution)/shard_map/all_gather | solution.py:75
  51.4 18.1 %all-to-all-start.3 = ((s32[8,1,192]{2,1,0:T(1,128)}), s32[8,1,192]{2,1,0:T(1,128)S(1)}, u32[]{:S(2)}, u32[]{:S(2)}) async-start(s32[8,1,192]{2,1,0:T(1,128)} %all_to_all.54), calls=%async_computation.3 | async-start | bytes 16384 | tf_op jit(solution)/shard_map/all_to_all | solution.py:79
  55.6 108.8 %reduce-scatter.2.cloned.1.call-start = ((), (), s32[]{:S(2)}) async-start(), calls=%async_computation.7 | async-start | bytes 40960 | tf_op jit(solution)/shard_map/reduce_scatter | solution.py:99
  82.8 31.5 %copy-start.2 = (s32[6144,1]{0,1:T(1,128)}, s32[6144,1]{0,1:T(1,128)S(1)}, u32[]{:S(2)}) copy-start(s32[6144,1]{0,1:T(1,128)S(1)} %compare_select_fusion.1) | copy-start | bytes 73732
  165.7 8.4 %all-to-all-start.4 = ((f32[8,1,192]{2,1,0:T(1,128)}), f32[8,1,192]{2,1,0:T(1,128)S(1)}, u32[]{:S(2)}, u32[]{:S(2)}) async-start(f32[8,1,192]{2,1,0:T(1,128)} %copy.69), calls=%async_computation.5 | async-start | bytes 16384 | tf_op jit(solution)/shard_map/all_to_all | solution.py:100
  174.2 27.5 %copy-start.3 = (s32[128,2,4]{0,2,1:T(4,128)S(1)}, s32[128,2,4]{0,2,1:T(4,128)}, u32[]{:S(2)}) copy-start(s32[128,2,4]{0,2,1:T(4,128)} %param.9) | copy-start | bytes 12292
  195.0 10.2 %all-to-all-start.1 = ((f32[8,1,192]{2,1,0:T(1,128)}), f32[8,1,192]{2,1,0:T(1,128)}, u32[]{:S(2)}, u32[]{:S(2)}) async-start(f32[8,1,192]{2,1,0:T(1,128)} %all_to_all.47), calls=%async_computation.1 | async-start | bytes 16384 | tf_op jit(solution)/shard_map/all_to_all | solution.py:78
  199.0 139.5 %all-reduce.2.cloned.1.call-start = ((), (), s32[]{:S(2)}) async-start(), calls=%async_computation.8 | async-start | bytes 4194304 | tf_op jit(solution)/shard_map/psum | solution.py:113
Sparse Core Ops, SparseCore 0:
  41.0 29.8 all-gather.4
  144.1 20.2 reduce-scatter.1
  206.0 132.4 all-reduce.1
where the time goes:
time: 376 us; the launch traced here: 374 us
  other arithmetic  110 us (29%)
  local copies, waits for them, and re-layouts  106 us (28%)
  blocking collectives  79.4 us (21%)
  waiting for transfers between devices  35.3 us (9%)
  starting transfers between devices  22 us (6%)
  between operations  16.6 us (4%)
  matrix products  4.43 us (1%)
    scatter-add x1, other arithmetic, local(): start.at[rows_flat].add(weight_flat[:, None] * cot_part.astype(jnp.float32))  53.2 us
    psum x1, blocking collectives, local(): total_sq = lax.psum(value_sq, ('dp', 'table')) + added_sq  39.2 us
    gather x1, local copies, waits for them, and re-layouts, local(): value_part = table_flat[rows_flat]  31.5 us
    gather x1, local copies, waits for them, and re-layouts, local(): cot_part = cot_all[position.reshape(-1)]  24.1 us
    mul x1, other arithmetic, local(): clip_factor * value_grad  22.5 us
    reduce_scatter x1, waiting for transfers between devices, local(): lax.psum_scatter(partial_dots, 'dp', scatter_dimension=0, tiled=True)[0]  18.3 us
    reduce_sum x1, other arithmetic, local(): value_sq = jnp.sum(value_grad * value_grad)  15.6 us
    all_gather x1, blocking collectives, local(): lax.all_gather(received[0], 'dp', axis=0, tiled=True)  13.7 us
  transfers between devices with their start and end apart: 8, of which 3 were waited for; matrix products, arithmetic and copies ran while one was open for 37% of the time, Pallas kernels for 0%

commit v1 on v0

v1 whole, which is shorter than its diff:
```python
import functools
import math

import jax
import jax.numpy as jnp
from jax import lax
from jax.experimental import pallas as pl
from jax.experimental.pallas import tpu as pltpu
from jax.sharding import PartitionSpec as P

limit_ratio = 5.0
BATCH = 8
MIB = 1024 * 1024


def split3(x):
    a = lax.reduce_precision(x, 8, 7)
    b = lax.reduce_precision(x - a, 8, 7)
    c = x - a - b
    return [t.astype(jnp.bfloat16) for t in (a, b, c)]


def digits(x, count):
    out = []
    for _ in range(count):
        out.append((x % 128).astype(jnp.bfloat16))
        x = x // 128
    return out


def join(rows):
    total = rows[0]
    for power, row in enumerate(rows[1:]):
        total = total + row * float(128 ** (power + 1))
    return total


def dots_kernel(rows_ref, pos_ref, values_ref, cot_ref, out_ref, table, partial):
    step = pl.program_id(0)
    chunk, columns = values_ref.shape
    piece = min(chunk, 256)

    @pl.loop(0, chunk // piece)
    def _(i):
        at = pl.multiple_of(i * piece, piece)
        to = pl.multiple_of(step * chunk + at, piece)
        table[pl.ds(to, piece), :] = values_ref[pl.ds(at, piece), :].astype(jnp.float32)

    @pl.when(step == pl.num_programs(0) - 1)
    def _():
        count = partial.shape[0]

        @pl.loop(0, count // (2 * BATCH))
        def _(b):
            base = pl.multiple_of(b * 2 * BATCH, 2 * BATCH)
            for u in range(2 * BATCH):
                row = rows_ref[base + u]
                pos = pos_ref[base + u]
                prod = table[pl.ds(row, 1), :] * cot_ref[pl.ds(pos, 1), :]
                total = prod[:, :128]
                for c in range(128, columns, 128):
                    total = total + prod[:, c : c + 128]
                partial[pl.ds(base + u, 1), :] = total

        ones = jnp.ones((8, 128), jnp.float32)
        width = 256

        @pl.loop(0, count // width)
        def _(i):
            at = pl.multiple_of(i * width, width)
            out_ref[:, pl.ds(at, width)] = lax.dot_general(
                ones,
                partial[pl.ds(at, width), :],
                (((1,), (1,)), ((), ())),
                precision=lax.Precision.HIGHEST,
                preferred_element_type=jnp.float32,
            )


def scatter_kernel(rows_ref, pos_ref, clash_ref, weight_ref, cot_ref, out_ref, sq_ref):
    total_rows, columns = out_ref.shape
    count = rows_ref.shape[0]
    batches = count // BATCH

    @pl.loop(0, total_rows // 128)
    def _(i):
        out_ref[pl.ds(pl.multiple_of(i * 128, 128), 128), :] = jnp.zeros((128, columns), jnp.float32)

    def term(b, u):
        at = u * batches + b
        return rows_ref[at], weight_ref[at] * cot_ref[pl.ds(pos_ref[at], 1), :]

    def fast(b, acc):
        terms = [term(b, u) for u in range(BATCH)]
        old = [out_ref[pl.ds(row, 1), :] for row, _ in terms]
        new = [o + t for o, (_, t) in zip(old, terms)]
        for (row, _), n in zip(terms, new):
            out_ref[pl.ds(row, 1), :] = n
        parts = [t * (o + n) for (_, t), o, n in zip(terms, old, new)]
        while len(parts) > 1:
            parts = [x + y for x, y in zip(parts[::2], parts[1::2])]
        return acc + parts[0]

    def slow(b, acc):
        for u in range(BATCH):
            row, t = term(b, u)
            o = out_ref[pl.ds(row, 1), :]
            n = o + t
            out_ref[pl.ds(row, 1), :] = n
            acc = acc + t * (o + n)
        return acc

    def body(b, acc):
        return lax.cond(clash_ref[b] == 0, functools.partial(fast, b), functools.partial(slow, b), acc)

    sq_ref[...] = lax.fori_loop(0, batches, body, jnp.zeros((1, columns), jnp.float32))


def scale_kernel(factor_ref, grad_ref, out_ref):
    out_ref[...] = grad_ref[...] * factor_ref[0]


def key_terms(dscore, query_half, key_index, key_count):
    labels = jnp.arange(key_count, dtype=jnp.int32)
    weighted = jnp.sum(
        jnp.where(key_index[:, :, :, None] == labels, dscore[:, :, :, None], 0.0), axis=2
    )
    return jnp.einsum(
        "thi,thc->hic", weighted, query_half.astype(jnp.float32), precision=lax.Precision.HIGHEST
    )


def pick_scores(query_half, keys, key_index):
    full = jnp.einsum("thc,hic->thi", query_half, keys, preferred_element_type=jnp.float32)
    labels = jnp.arange(keys.shape[1], dtype=jnp.int32)
    return jnp.sum(jnp.where(key_index[:, :, :, None] == labels, full[:, :, None, :], 0.0), axis=3)


def local(queries, sub_keys, values, slot_first, slot_second, cotangent):
    table_size = lax.axis_size("table")
    data_size = lax.axis_size("dp")
    devices = data_size * table_size
    token_count, head_count, pick_count = slot_first.shape
    half_width = queries.shape[2] // 2
    key_count = sub_keys.shape[2]
    first_block, _, column_count = values.shape
    slot_count = token_count * head_count * pick_count
    capacity = 3 * slot_count // (2 * table_size)
    table_rows = first_block * key_count
    all_tokens = token_count * devices
    both = ("dp", "table")

    cot_columns = lax.all_to_all(cotangent, "dp", split_axis=1, concat_axis=0, tiled=True)
    cot_all = lax.all_gather(cot_columns, "table", axis=0, tiled=True)

    query_first = queries[:, :, :half_width]
    query_second = queries[:, :, half_width:]
    raw_score = pick_scores(query_first, sub_keys[0], slot_first)
    raw_score = raw_score + pick_scores(query_second, sub_keys[1], slot_second)
    exp_score = jnp.exp(raw_score)
    weight = exp_score / jnp.sum(exp_score, axis=2, keepdims=True)

    first_flat = slot_first.reshape(slot_count)
    second_flat = slot_second.reshape(slot_count)
    owner = first_flat // first_block
    local_row = first_flat % first_block * key_count + second_flat
    token_row = jnp.arange(slot_count, dtype=jnp.int32) // (head_count * pick_count)
    groups = jnp.arange(table_size, dtype=jnp.int32)
    slots = jnp.arange(slot_count, dtype=jnp.int32)
    member = (groups[:, None] == owner[None, :]).astype(jnp.bfloat16)
    earlier = (slots[:, None] < slots[None, :]).astype(jnp.bfloat16)
    ahead = jnp.dot(member, earlier, preferred_element_type=jnp.float32)
    before = jnp.sum(ahead * member.astype(jnp.float32), axis=0).astype(jnp.int32)
    target = owner * capacity + before
    place = (
        target[:, None] == jnp.arange(table_size * capacity, dtype=jnp.int32)[None, :]
    ).astype(jnp.bfloat16)
    fields = jnp.stack(
        split3(weight.reshape(slot_count))
        + digits(local_row, 3)
        + digits(token_row, 2)
        + [jnp.ones((slot_count,), jnp.bfloat16)]
    )
    placed = jnp.dot(fields, place, preferred_element_type=jnp.float32)
    filler = (jnp.arange(table_size * capacity, dtype=jnp.int32) % table_rows).astype(jnp.float32)
    send = jnp.stack(
        [
            placed[0] + placed[1] + placed[2],
            jnp.where(placed[8] > 0.5, join([placed[3], placed[4], placed[5]]), filler),
            join([placed[6], placed[7]]),
        ]
    )
    send = send.reshape(3, table_size, capacity).transpose(1, 0, 2).reshape(1, table_size, 3 * capacity)
    send = jnp.broadcast_to(send, (data_size, table_size, 3 * capacity)).reshape(devices, 3 * capacity)
    records = lax.all_to_all(send, both, split_axis=0, concat_axis=0, tiled=True)
    records = records.reshape(devices, 3, capacity)
    source = jnp.arange(devices, dtype=jnp.int32)[:, None]
    base = (source % table_size * data_size + source // table_size) * token_count
    count = devices * capacity
    weight_flat = records[:, 0].reshape(count)
    rows_flat = records[:, 1].astype(jnp.int32).reshape(count)
    pos_flat = (records[:, 2].astype(jnp.int32) + base).reshape(count)

    cot_wide = cot_all.astype(jnp.float32)
    smem = pl.BlockSpec(memory_space=pltpu.SMEM)
    chunk = min(2048, table_rows)
    dots = pl.pallas_call(
        dots_kernel,
        grid=(table_rows // chunk,),
        out_shape=jax.ShapeDtypeStruct((8, count), jnp.float32),
        in_specs=[
            smem,
            smem,
            pl.BlockSpec((chunk, column_count), lambda i: (i, 0)),
            pl.BlockSpec((all_tokens, column_count), lambda i: (0, 0), pipeline_mode=pl.Buffered(1)),
        ],
        out_specs=pl.BlockSpec((8, count), lambda i: (0, 0)),
        scratch_shapes=[
            pltpu.VMEM((table_rows, column_count), jnp.float32),
            pltpu.VMEM((count, 128), jnp.float32),
        ],
        compiler_params=pltpu.CompilerParams(vmem_limit_bytes=58 * MIB),
        name="slot_dots",
    )(rows_flat, pos_flat, values.reshape(table_rows, column_count), cot_wide)
    partial_dots = dots[0].reshape(devices, capacity)
    returned = lax.all_to_all(partial_dots, both, split_axis=0, concat_axis=0, tiled=True)
    returned = jnp.sum(returned.reshape(data_size, table_size * capacity), axis=0)
    picked = jnp.sum(
        lax.dot_general(
            jnp.stack(split3(returned)),
            place,
            (((1,), (1,)), ((), ())),
            preferred_element_type=jnp.float32,
        ),
        axis=0,
    ).reshape(token_count, head_count, pick_count)
    dscore = weight * (picked - jnp.sum(weight * picked, axis=2, keepdims=True))
    key_grad = jnp.stack(
        [
            key_terms(dscore, query_first, slot_first, key_count),
            key_terms(dscore, query_second, slot_second, key_count),
        ]
    )
    by_batch = rows_flat.reshape(BATCH, count // BATCH)
    clash = jnp.zeros((count // BATCH,), jnp.bool_)
    for u in range(BATCH):
        for v in range(u):
            clash = clash | (by_batch[u] == by_batch[v])
    clash = clash.astype(jnp.int32)
    weight_flat, key_grad = lax.optimization_barrier((weight_flat, key_grad))
    key_part = lax.psum_scatter(key_grad, both, scatter_dimension=2, tiled=True)

    value_grad, value_sq = pl.pallas_call(
        scatter_kernel,
        out_shape=(
            jax.ShapeDtypeStruct((table_rows, column_count), jnp.float32),
            jax.ShapeDtypeStruct((1, column_count), jnp.float32),
        ),
        in_specs=[smem, smem, smem, smem, pl.BlockSpec(memory_space=pltpu.VMEM)],
        out_specs=(
            pl.BlockSpec(memory_space=pltpu.VMEM),
            pl.BlockSpec(memory_space=pltpu.VMEM),
        ),
        compiler_params=pltpu.CompilerParams(vmem_limit_bytes=58 * MIB),
        cost_estimate=pl.CostEstimate(
            flops=2 * count * column_count,
            bytes_accessed=6 * 4 * table_rows * column_count,
            transcendentals=0,
        ),
        name="value_scatter",
    )(rows_flat, pos_flat, clash, weight_flat, cot_wide)

    own_sq = jnp.sum(value_sq) + jnp.sum(key_part * key_part)
    all_sq = lax.all_to_all(
        jnp.broadcast_to(own_sq, (devices, 128)), both, split_axis=0, concat_axis=0, tiled=True
    )
    total_sq = jnp.sum(all_sq[:, 0])
    clip_factor = jnp.minimum(1.0, limit_ratio * math.sqrt(all_tokens) / jnp.sqrt(total_sq))
    clip_factor = clip_factor.reshape(1)
    value_update = pl.pallas_call(
        scale_kernel,
        grid=(table_rows // chunk,),
        out_shape=jax.ShapeDtypeStruct((table_rows, column_count), jnp.float32),
        in_specs=[smem, pl.BlockSpec((chunk, column_count), lambda i: (i, 0))],
        out_specs=pl.BlockSpec((chunk, column_count), lambda i: (i, 0)),
        compiler_params=pltpu.CompilerParams(vmem_limit_bytes=32 * MIB),
        name="value_scale",
    )(clip_factor, value_grad).reshape(first_block, key_count, column_count)
    key_update = clip_factor * key_part
    return (value_update, key_update, clip_factor)


def solution(mesh):
    placed = (
        P(("dp", "table"), None, None),
        P(),
        P("table", None, "dp"),
        P(("dp", "table"), None, None),
        P(("dp", "table"), None, None),
        P(("dp", "table"), None),
    )
    return jax.shard_map(
        local,
        mesh=mesh,
        in_specs=placed,
        out_specs=(P("table", None, "dp"), P(None, None, ("dp", "table"), None), P()),
        check_vma=False,
    )
```

time: 376 us -> 299 us (0.80)
  Pallas kernels: 0 us -> 134 us
  other arithmetic: 110 us -> 13.5 us
  local copies, waits for them, and re-layouts: 106 us -> 10.4 us
  blocking collectives: 79.4 us -> 23.9 us
  waiting for transfers between devices: 35.3 us -> 86.6 us
  starting transfers between devices: 22 us -> 8.4 us
    pallas_call x0 -> x3, Pallas kernels: none -> 134 us  [the longest x1 63 us: local(): pl.pallas_call(scatter_kernel, out_shape=(jax.ShapeDtypeStruct((table_row...]
    gather x7 -> x0, local copies, waits for them, and re-layouts: 78.8 us -> none  [the longest x1 31.5 us: local(): value_part = table_flat[rows_flat]]
    scatter-add x1 -> x0, other arithmetic: 53.2 us -> none  [local(): start.at[rows_flat].add(weight_flat[:, None] * cot_part.astype(jnp.float32))]
    reduce_scatter x1, waiting for transfers between devices: 18.3 us -> 66.8 us  [local(): key_part = lax.psum_scatter(key_grad, both, scatter_dimension=2, tiled=True)]
    all_gather x3 -> x0, blocking collectives: 40.2 us -> none  [the longest x1 13.7 us: local(): lax.all_gather(received[0], 'dp', axis=0, tiled=True)]
    psum x1 -> x0, blocking collectives: 39.2 us -> none  [local(): total_sq = lax.psum(value_sq, ('dp', 'table')) + added_sq]
    all_to_all x0 -> x2, blocking collectives: none -> 23.9 us  [the longest x1 15.1 us: local(): lax.all_to_all(cotangent, 'dp', split_axis=1, concat_axis=0, tiled=True)]
    mul x3 -> x1, other arithmetic: 23.2 us -> 0.01 us  [local(): (source % table_size * data_size + source // table_size) * token_count]
  transfers between devices with their start and end apart: 8 -> 4, of which waited for: 3 -> 4; matrix products, arithmetic and copies ran while one was open for 37% -> 4% of each run, Pallas kernels for 0% -> 21%
where the time goes in v1:
time: 299 us
  Pallas kernels  134 us (45%)
  waiting for transfers between devices  86.6 us (29%)
  blocking collectives  23.9 us (8%)
  between operations  17.5 us (6%)
  other arithmetic  13.5 us (5%)
  local copies, waits for them, and re-layouts  10.4 us (3%)
  starting transfers between devices  8.4 us (3%)
  matrix products  4.64 us (2%)
    reduce_scatter x1, waiting for transfers between devices, local(): key_part = lax.psum_scatter(key_grad, both, scatter_dimension=2, tiled=True)  66.8 us
    pallas_call x1, Pallas kernels, local(): pl.pallas_call(scatter_kernel, out_shape=(jax.ShapeDtypeStruct((table_row...  63 us
    pallas_call x1, Pallas kernels, local(): pl.pallas_call(dots_kernel, grid=(table_rows // chunk,), out_shape=jax.Sh...  43.4 us
    pallas_call x1, Pallas kernels, local(): pl.pallas_call(scale_kernel, grid=(table_rows // chunk,), out_shape=jax.S...  27.2 us
    all_to_all x1, blocking collectives, local(): lax.all_to_all(cotangent, 'dp', split_axis=1, concat_axis=0, tiled=True)  15.1 us
    all_to_all x1, blocking collectives, local(): lax.all_to_all(jnp.broadcast_to(own_sq, (devices, 128)), both, split_axis...  8.84 us
    all_to_all x1, waiting for transfers between devices, local(): lax.all_to_all(send, both, split_axis=0, concat_axis=0, tiled=True)  7.44 us
    all_to_all x1, waiting for transfers between devices, local(): lax.all_to_all(partial_dots, both, split_axis=0, concat_axis=0, tiled=True)  6.4 us
  transfers between devices with their start and end apart: 4, of which 4 were waited for; matrix products, arithmetic and copies ran while one was open for 4% of the time, Pallas kernels for 21%

profile of v1, /device:TPU:0, one launch (start us, length us, event | category | flops | bytes accessed | tf_op | source)
XLA Modules:
  0.0 298.7 jit_solution(16521649875691557446)
XLA Ops:
  7.2 1.1 copy.93
  8.3 15.1 %all_to_all.47 = bf16[128,4,256]{2,0,1:T(8,128)(2,1)} all-to-all(bf16[128,4,256]{2,0,1:T(8,128)(2,1)S(1)} %bitcast.33), channel_id=1, replica_groups=mesh['dp'=4,'table'=8] {'dp'}, dimensions={1} | all-to-all | bytes 524288 | tf_op jit(solution)/shard_map/all_to_all | solution.py:153
  23.4 0.8 copy.65
  24.6 0.8 copy.66
  26.9 1.0 select_reduce_fusion.2
  29.0 1.2 fusion.1
  30.7 0.7 all_to_all.32
  31.4 3.7 %all-to-all-start = ((f32[32,1,576]{2,1,0:T(1,128)}), f32[32,1,576]{2,1,0:T(1,128)S(1)}, u32[]{:S(2)}, u32[]{:S(2)}) async-start(f32[32,1,576]{2,1,0:T(1,128)} %all_to_all.32), calls=%async_computation | async-start | bytes 163840 | tf_op jit(solution)/shard_map/all_to_all | solution.py:195
  35.3 7.4 %all-to-all-done = f32[32,1,576]{2,1,0:T(1,128)S(1)} async-done(((f32[32,1,576]{2,1,0:T(1,128)}), f32[32,1,576]{2,1,0:T(1,128)S(1)}, u32[]{:S(2)}, u32[]{:S(2)}) %all-to-all-start) | async-done | bytes 73760 | tf_op jit(solution)/shard_map/all_to_all | solution.py:195
  44.6 6.0 %all-gather.2.cloned.1.call-done = bf16[4096,256]{1,0:T(8,128)(2,1)} async-done(((bf16[512,256]{1,0:T(8,128)(2,1)}), bf16[4096,256]{1,0:T(8,128)(2,1)}) %all-gather.2.cloned.1.call-update) | async-done | bytes 2097168 | tf_op jit(solution)/shard_map/all_gather | solution.py:154
  50.6 3.9 %convert_element_type.175.cot_ref = f32[4096,256]{1,0:T(8,128)} convert(bf16[4096,256]{1,0:T(8,128)(2,1)} %all-gather.2.cloned.1.call-done) | non-fusion elementwise | flops 1048576 | bytes 6291456 | tf_op jit(solution)/shard_map/convert_element_type | solution.py:204
  54.5 43.4 %slot_dots.1 = f32[8,6144]{1,0:T(8,128)} custom-call(s32[6144]{0:T(1024)} %convert_element_type.171.rows_ref, s32[6144]{0:T(1024)} %add.267.pos_ref, bf16[32768,256]{1,0:T(8,128)(2,1)} %bitcast.31, f32[4096,256]{1,0:T(8,128)} %convert_element_type.175.cot_ref), custom_call_target="tpu_custom_call" | custom-call | tf_op jit(solution)/shard_map/slot_dots/pallas_call | solution.py:207
  97.9 1.0 slice_reduce_fusion.1
  98.9 0.7 all_to_all.42
  99.6 4.6 %all-to-all-start.2 = ((f32[32,1,192]{2,1,0:T(1,128)}), f32[32,1,192]{2,1,0:T(1,128)S(1)}, u32[]{:S(2)}, u32[]{:S(2)}) async-start(f32[32,1,192]{2,1,0:T(1,128)} %all_to_all.42), calls=%async_computation.2 | async-start | bytes 65536 | tf_op jit(solution)/shard_map/all_to_all | solution.py:226
  105.1 6.4 %all-to-all-done.2 = f32[32,1,192]{2,1,0:T(1,128)S(1)} async-done(((f32[32,1,192]{2,1,0:T(1,128)}), f32[32,1,192]{2,1,0:T(1,128)S(1)}, u32[]{:S(2)}, u32[]{:S(2)}) %all-to-all-start.2) | async-done | bytes 24608 | tf_op jit(solution)/shard_map/all_to_all | solution.py:226
  111.7 1.3 fusion.7
  115.3 1.5 pad_maximum_fusion
  118.8 63.0 %value_scatter.1 = (f32[32768,256]{1,0:T(8,128)}, f32[1,256]{1,0:T(1,128)}) custom-call(s32[6144]{0:T(1024)} %convert_element_type.171.rows_ref, s32[6144]{0:T(1024)} %add.267.pos_ref, s32[768]{0:T(1024)} %or_convert_fusion.clash_ref, f32[6144]{0:T(1024)} %reshape_squeeze.4.weight_ref, f32[4096,256]{1,0:T(8,128)} %convert_element_type.175.cot_ref), custom_call_target="tpu_custom_call" | custom-call | flops 3145728 | bytes 201326592 | tf_op jit(solution)/shard_map/value_scatter/pallas_call | solution.py:253
  181.9 1.3 reduce_sum.120
  183.1 66.8 %reduce-scatter.2.cloned.1.call-done = f32[2,2,16,256]{3,2,1,0:T(8,128)} async-done(((f32[2,2,512,256]{3,2,1,0:T(8,128)}), f32[2,2,16,256]{3,2,1,0:T(8,128)}) %reduce-scatter.2.cloned.1.call-update) | async-done | bytes 65552 | tf_op jit(solution)/shard_map/reduce_scatter | solution.py:251
  249.9 1.5 multiply_reduce_fusion
  252.7 8.8 %all_to_all.48 = f32[32,1,128]{2,1,0:T(1,128)S(1)} all-to-all(f32[32,1,128]{2,1,0:T(1,128)S(1)} %broadcast_in_dim.69), channel_id=1, replica_groups=mesh['dp'=4,'table'=8] {'dp','table'}, dimensions={0} | all-to-all | bytes 32768 | tf_op jit(solution)/shard_map/all_to_all | solution.py:274
  262.8 27.2 %value_scale.1 = f32[32768,256]{1,0:T(8,128)} custom-call(f32[1]{0:T(128)} %bitcast.11.factor_ref, f32[32768,256]{1,0:T(8,128)} %get-tuple-element.10.grad_ref), custom_call_target="tpu_custom_call" | custom-call | tf_op jit(solution)/shard_map/value_scale/pallas_call | solution.py:280
  (84 shorter events, 11.9 us)
Async XLA Ops:
  7.2 18.5 %copy-start.1 = (bf16[128,2,512]{2,1,0:T(2,128)(2,1)S(1)}, bf16[128,2,512]{2,1,0:T(2,128)(2,1)}, u32[]{:S(2)}) copy-start(bf16[128,2,512]{2,1,0:T(2,128)(2,1)} %param.6) | copy-start | bytes 786436
  7.2 18.7 %copy-start = (bf16[2,2,512,256]{3,2,1,0:T(8,128)(2,1)S(1)}, bf16[2,2,512,256]{3,2,1,0:T(8,128)(2,1)}, u32[]{:S(2)}) copy-start(bf16[2,2,512,256]{3,2,1,0:T(8,128)(2,1)} %param.7) | copy-start | bytes 3145732
  7.2 43.4 %all-gather.2.cloned.1.call-start = ((), (), s32[]{:S(2)}) async-start(), calls=%async_computation.5 | async-start | bytes 2359296 | tf_op jit(solution)/shard_map/all_gather | solution.py:154
  25.9 1.0 copy-start.3
  25.9 1.0 copy-start.4
  31.4 11.3 %all-to-all-start = ((f32[32,1,576]{2,1,0:T(1,128)}), f32[32,1,576]{2,1,0:T(1,128)S(1)}, u32[]{:S(2)}, u32[]{:S(2)}) async-start(f32[32,1,576]{2,1,0:T(1,128)} %all_to_all.32), calls=%async_computation | async-start | bytes 163840 | tf_op jit(solution)/shard_map/all_to_all | solution.py:195
  99.6 11.9 %all-to-all-start.2 = ((f32[32,1,192]{2,1,0:T(1,128)}), f32[32,1,192]{2,1,0:T(1,128)S(1)}, u32[]{:S(2)}, u32[]{:S(2)}) async-start(f32[32,1,192]{2,1,0:T(1,128)} %all_to_all.42), calls=%async_computation.2 | async-start | bytes 65536 | tf_op jit(solution)/shard_map/all_to_all | solution.py:226
  104.2 145.7 %reduce-scatter.2.cloned.1.call-start = ((), (), s32[]{:S(2)}) async-start(), calls=%async_computation.6 | async-start | bytes 2162688 | tf_op jit(solution)/shard_map/reduce_scatter | solution.py:251
  262.8 27.3 %copy-start.2 = (f32[2,2,16,256]{3,2,1,0:T(8,128)S(1)}, f32[2,2,16,256]{3,2,1,0:T(8,128)}, u32[]{:S(2)}) copy-start(f32[2,2,16,256]{3,2,1,0:T(8,128)} %reduce-scatter.2.cloned.1.call-done) | copy-start | bytes 196612
Sparse Core Ops, SparseCore 0:
  23.5 26.9 all-gather.1
  116.9 132.9 reduce-scatter.1

commit v2 on v1

--- a/solution.py
+++ b/solution.py
@@ -118,6 +118,128 @@
 
 def scale_kernel(factor_ref, grad_ref, out_ref):
     out_ref[...] = grad_ref[...] * factor_ref[0]
+
+
+def partner_of(axis, bit):
+    at = lax.axis_index(axis)
+    upper = (at // bit) % 2
+    return upper, {axis: at + bit * (1 - 2 * upper)}
+
+
+def chunk_of(slot, plan, table_size):
+    chunk = 0
+    for level, (axis, bit) in enumerate(plan):
+        if (slot >> (len(plan) - 1 - level)) & 1:
+            chunk += bit * (table_size if axis == "dp" else 1)
+    return chunk
+
+
+def reduce_kernel(
+    plans, table_size, key_ref, value_sq_ref, out_ref, total_ref,
+    held, inbox, sums, sums_in, send_sem, recv_sem, sum_send, sum_recv,
+):
+    levels = len(plans[0])
+    chunks = 2**levels
+    share = out_ref.shape[1]
+    barrier = pltpu.get_barrier_semaphore()
+    for axis, bit in plans[0]:
+        _, where = partner_of(axis, bit)
+        pl.semaphore_signal(barrier, inc=1, device_id=where, device_id_type=pl.DeviceIdType.MESH)
+    for lane, plan in enumerate(plans):
+        for slot in range(chunks):
+            row = chunk_of(slot, plan, table_size) * share
+            for q in range(out_ref.shape[0]):
+                held[lane, slot, q * share : (q + 1) * share, :] = key_ref[
+                    q, row : row + share, lane * 128 : (lane + 1) * 128
+                ]
+    pl.semaphore_wait(barrier, levels)
+
+    offsets = [0] * len(plans)
+    for level in range(levels):
+        size = chunks >> (level + 1)
+        copies = []
+        for lane, plan in enumerate(plans):
+            upper, where = partner_of(*plan[level])
+            give = offsets[lane] + (1 - upper) * size
+            offsets[lane] = offsets[lane] + upper * size
+            copy = pltpu.make_async_remote_copy(
+                src_ref=held.at[lane, pl.ds(give, size)],
+                dst_ref=inbox.at[lane, pl.ds(size, size)],
+                send_sem=send_sem.at[lane, level],
+                recv_sem=recv_sem.at[lane, level],
+                device_id=where,
+                device_id_type=pl.DeviceIdType.MESH,
+            )
+            copy.start()
+            copies.append(copy)
+        for lane, copy in enumerate(copies):
+            copy.wait()
+            keep = offsets[lane]
+
+            @pl.loop(0, size)
+            def _(i):
+                held[lane, keep + i] = held[lane, keep + i] + inbox[lane, size + i]
+
+    own = jnp.sum(value_sq_ref[...])
+    for lane in range(len(plans)):
+        part = held[lane, offsets[lane]]
+        own = own + jnp.sum(part * part)
+        for q in range(out_ref.shape[0]):
+            out_ref[q, :, lane * 128 : (lane + 1) * 128] = part[q * share : (q + 1) * share, :]
+    sums[0] = jnp.full((8, 128), own, jnp.float32)
+    for level in range(levels):
+        _, where = partner_of(*plans[0][level])
+        copy = pltpu.make_async_remote_copy(
+            src_ref=sums.at[level],
+            dst_ref=sums_in.at[level],
+            send_sem=sum_send.at[level],
+            recv_sem=sum_recv.at[level],
+            device_id=where,
+            device_id_type=pl.DeviceIdType.MESH,
+        )
+        copy.start()
+        copy.wait()
+        sums[level + 1] = sums[level] + sums_in[level]
+    total_ref[...] = sums[levels]
+
+
+def reduce_keys(key_grad, value_sq, data_size, table_size):
+    chunks = data_size * table_size
+    kinds, heads, key_count, width = key_grad.shape
+    share = key_count // chunks
+    table_bits = [2**i for i in range(table_size.bit_length() - 1)]
+    data_part = [("dp", 2**i) for i in range(data_size.bit_length() - 1)]
+    plans = []
+    for lane in range(width // 128):
+        rest = table_bits[1:] if lane % 2 == 0 else table_bits[:0:-1]
+        plans.append([("table", b) for b in table_bits[:1] + rest] + data_part)
+    lanes, levels = len(plans), len(plans[0])
+    parts = kinds * heads
+    vmem = pl.BlockSpec(memory_space=pltpu.VMEM)
+    key_part, total = pl.pallas_call(
+        functools.partial(reduce_kernel, plans, table_size),
+        out_shape=(
+            jax.ShapeDtypeStruct((parts, share, width), jnp.float32),
+            jax.ShapeDtypeStruct((8, 128), jnp.float32),
+        ),
+        in_specs=[vmem, vmem],
+        out_specs=(vmem, vmem),
+        scratch_shapes=[
+            pltpu.VMEM((lanes, chunks, parts * share, 128), jnp.float32),
+            pltpu.VMEM((lanes, chunks, parts * share, 128), jnp.float32),
+            pltpu.VMEM((levels + 1, 8, 128), jnp.float32),
+            pltpu.VMEM((levels, 8, 128), jnp.float32),
+            pltpu.SemaphoreType.DMA((lanes, levels)),
+            pltpu.SemaphoreType.DMA((lanes, levels)),
+            pltpu.SemaphoreType.DMA((levels,)),
+            pltpu.SemaphoreType.DMA((levels,)),
+        ],
+        compiler_params=pltpu.CompilerParams(
+            collective_id=0, has_side_effects=True, vmem_limit_bytes=24 * MIB
+        ),
+        name="key_reduce",
+    )(key_grad.reshape(parts, key_count, width), value_sq)
+    return key_part.reshape(kinds, heads, share, width), total[0, 0]
 
 
 def key_terms(dscore, query_half, key_index, key_count):
@@ -247,9 +369,6 @@
         for v in range(u):
             clash = clash | (by_batch[u] == by_batch[v])
     clash = clash.astype(jnp.int32)
-    weight_flat, key_grad = lax.optimization_barrier((weight_flat, key_grad))
-    key_part = lax.psum_scatter(key_grad, both, scatter_dimension=2, tiled=True)
-
     value_grad, value_sq = pl.pallas_call(
         scatter_kernel,
         out_shape=(
@@ -270,11 +389,7 @@
         name="value_scatter",
     )(rows_flat, pos_flat, clash, weight_flat, cot_wide)
 
-    own_sq = jnp.sum(value_sq) + jnp.sum(key_part * key_part)
-    all_sq = lax.all_to_all(
-        jnp.broadcast_to(own_sq, (devices, 128)), both, split_axis=0, concat_axis=0, tiled=True
-    )
-    total_sq = jnp.sum(all_sq[:, 0])
+    key_part, total_sq = reduce_keys(key_grad, value_sq, data_size, table_size)
     clip_factor = jnp.minimum(1.0, limit_ratio * math.sqrt(all_tokens) / jnp.sqrt(total_sq))
     clip_factor = clip_factor.reshape(1)
     value_update = pl.pallas_call(

time: 299 us -> 251 us (0.84)
  waiting for transfers between devices: 86.6 us -> 20.5 us
  Pallas kernels: 134 us -> 172 us
  blocking collectives: 23.9 us -> 0 us
  starting transfers between devices: 8.4 us -> 14.6 us
  other arithmetic: 13.5 us -> 8.78 us
  local copies, waits for them, and re-layouts: 10.4 us -> 13.8 us
    reduce_scatter x1 -> x0, waiting for transfers between devices: 66.8 us -> none  [local(): key_part = lax.psum_scatter(key_grad, both, scatter_dimension=2, tiled=True)]
    pallas_call x0 -> x1, Pallas kernels: none -> 38.2 us  [reduce_keys(): pl.pallas_call(functools.partial(reduce_kernel, plans, table_size), out_s...]
    all_to_all x2 -> x0, blocking collectives: 23.9 us -> none  [the longest x1 15.1 us: local(): lax.all_to_all(cotangent, 'dp', split_axis=1, concat_axis=0, tiled=True)]
    all_to_all x1, waiting for transfers between devices: 6.4 us -> 0.01 us  [local(): lax.all_to_all(partial_dots, both, split_axis=0, concat_axis=0, tiled=True)]
    all_to_all x0 -> x1, starting transfers between devices: none -> 6.32 us  [local(): lax.all_to_all(cotangent, 'dp', split_axis=1, concat_axis=0, tiled=True)]
    all_to_all x0 -> x1, waiting for transfers between devices: none -> 5.47 us  [local(): lax.all_to_all(cotangent, 'dp', split_axis=1, concat_axis=0, tiled=True)]
    reduce_sum x3 -> x0, other arithmetic: 3.33 us -> none  [the longest x2 2.73 us: local(): own_sq = jnp.sum(value_sq) + jnp.sum(key_part * key_part)]
  transfers between devices with their start and end apart: 4 -> 4, of which waited for: 4 -> 3; matrix products, arithmetic and copies ran while one was open for 4% -> 5% of each run, Pallas kernels for 21% -> 25%
where the time goes in v2:
time: 251 us; the launch traced here: 250 us
  Pallas kernels  172 us (69%)
  waiting for transfers between devices  20.5 us (8%)
  between operations  16.2 us (6%)
  starting transfers between devices  14.6 us (6%)
  local copies, waits for them, and re-layouts  13.8 us (5%)
  other arithmetic  8.78 us (3%)
  matrix products  4.65 us (2%)
    pallas_call x1, Pallas kernels, local(): pl.pallas_call(scatter_kernel, out_shape=(jax.ShapeDtypeStruct((table_row...  63 us
    pallas_call x1, Pallas kernels, local(): pl.pallas_call(dots_kernel, grid=(table_rows // chunk,), out_shape=jax.Sh...  43.4 us
    pallas_call x1, Pallas kernels, reduce_keys(): pl.pallas_call(functools.partial(reduce_kernel, plans, table_size), out_s...  38.2 us
    pallas_call x1, Pallas kernels, local(): pl.pallas_call(scale_kernel, grid=(table_rows // chunk,), out_shape=jax.S...  27.2 us
    all_gather x1, waiting for transfers between devices, local(): cot_all = lax.all_gather(cot_columns, 'table', axis=0, tiled=True)  7.61 us
    all_to_all x1, waiting for transfers between devices, local(): lax.all_to_all(send, both, split_axis=0, concat_axis=0, tiled=True)  7.44 us
    all_to_all x1, starting transfers between devices, local(): lax.all_to_all(cotangent, 'dp', split_axis=1, concat_axis=0, tiled=True)  6.32 us
    all_to_all x1, waiting for transfers between devices, local(): lax.all_to_all(cotangent, 'dp', split_axis=1, concat_axis=0, tiled=True)  5.47 us
  transfers between devices with their start and end apart: 4, of which 3 were waited for; matrix products, arithmetic and copies ran while one was open for 5% of the time, Pallas kernels for 25%

profile of v2, /device:TPU:0, one launch (start us, length us, event | category | flops | bytes accessed | tf_op | source)
XLA Modules:
  0.0 250.3 jit_solution(10128359314323596122)
XLA Ops:
  7.2 1.8 copy.74
  8.9 6.3 %all-to-all-start.1 = ((bf16[128,4,256]{2,0,1:T(8,128)(2,1)}), bf16[128,4,256]{2,0,1:T(8,128)(2,1)S(1)}, u32[]{:S(2)}, u32[]{:S(2)}) async-start(bf16[128,4,256]{2,0,1:T(8,128)(2,1)} %bitcast.31), calls=%async_computation.1 | async-start | bytes 524288 | tf_op jit(solution)/shard_map/all_to_all | solution.py:275
  15.3 0.8 copy.48
  16.5 0.8 copy.49
  17.5 1.2 fusion.51
  18.7 5.5 %all-to-all-done.1 = bf16[128,4,256]{2,0,1:T(8,128)(2,1)S(1)} async-done(((bf16[128,4,256]{2,0,1:T(8,128)(2,1)}), bf16[128,4,256]{2,0,1:T(8,128)(2,1)S(1)}, u32[]{:S(2)}, u32[]{:S(2)}) %all-to-all-start.1) | async-done | bytes 262176 | tf_op jit(solution)/shard_map/all_to_all | solution.py:275
  24.2 0.7 copy-done.2
  26.0 1.0 select_reduce_fusion.2
  28.0 1.2 fusion.1
  29.7 0.7 all_to_all.26
  30.4 3.7 %all-to-all-start = ((f32[32,1,576]{2,1,0:T(1,128)}), f32[32,1,576]{2,1,0:T(1,128)S(1)}, u32[]{:S(2)}, u32[]{:S(2)}) async-start(f32[32,1,576]{2,1,0:T(1,128)} %all_to_all.26), calls=%async_computation | async-start | bytes 163840 | tf_op jit(solution)/shard_map/all_to_all | solution.py:317
  34.2 7.4 %all-to-all-done = f32[32,1,576]{2,1,0:T(1,128)S(1)} async-done(((f32[32,1,576]{2,1,0:T(1,128)}), f32[32,1,576]{2,1,0:T(1,128)S(1)}, u32[]{:S(2)}, u32[]{:S(2)}) %all-to-all-start) | async-done | bytes 73760 | tf_op jit(solution)/shard_map/all_to_all | solution.py:317
  43.8 0.7 convert_element_type.171.rows_ref
  45.1 7.6 %all-gather.2.cloned.1.call-done = bf16[4096,256]{1,0:T(8,128)(2,1)} async-done(((bf16[512,256]{1,0:T(8,128)(2,1)}), bf16[4096,256]{1,0:T(8,128)(2,1)}) %all-gather.2.cloned.1.call-update) | async-done | bytes 2097168 | tf_op jit(solution)/shard_map/all_gather | solution.py:276
  52.7 3.9 %convert_element_type.174.cot_ref = f32[4096,256]{1,0:T(8,128)} convert(bf16[4096,256]{1,0:T(8,128)(2,1)} %all-gather.2.cloned.1.call-done) | non-fusion elementwise | flops 1048576 | bytes 6291456 | tf_op jit(solution)/shard_map/convert_element_type | solution.py:326
  56.6 43.4 %slot_dots.1 = f32[8,6144]{1,0:T(8,128)} custom-call(s32[6144]{0:T(1024)} %convert_element_type.171.rows_ref, s32[6144]{0:T(1024)} %add.262.pos_ref, bf16[32768,256]{1,0:T(8,128)(2,1)} %bitcast.34, f32[4096,256]{1,0:T(8,128)} %convert_element_type.174.cot_ref), custom_call_target="tpu_custom_call" | custom-call | tf_op jit(solution)/shard_map/slot_dots/pallas_call | solution.py:329
  100.1 1.0 slice_reduce_fusion.1
  101.0 0.7 all_to_all.34
  101.8 4.6 %all-to-all-start.2 = ((f32[32,1,192]{2,1,0:T(1,128)}), f32[32,1,192]{2,1,0:T(1,128)S(1)}, u32[]{:S(2)}, u32[]{:S(2)}) async-start(f32[32,1,192]{2,1,0:T(1,128)} %all_to_all.34), calls=%async_computation.2 | async-start | bytes 65536 | tf_op jit(solution)/shard_map/all_to_all | solution.py:348
  107.0 0.7 reshape_squeeze.4.weight_ref
  107.6 63.0 %value_scatter.1 = (f32[32768,256]{1,0:T(8,128)}, f32[1,256]{1,0:T(1,128)}) custom-call(s32[6144]{0:T(1024)} %convert_element_type.171.rows_ref, s32[6144]{0:T(1024)} %add.262.pos_ref, s32[768]{0:T(1024)} %or_convert_fusion.clash_ref, f32[6144]{0:T(1024)} %reshape_squeeze.4.weight_ref, f32[4096,256]{1,0:T(8,128)} %convert_element_type.174.cot_ref), custom_call_target="tpu_custom_call" | custom-call | flops 3145728 | bytes 201326592 | tf_op jit(solution)/shard_map/value_scatter/pallas_call | solution.py:372
  170.8 1.3 fusion.7
  175.0 38.2 %key_reduce.1 = (f32[4,16,256]{2,1,0:T(8,128)S(1)}, f32[8,128]{1,0:T(8,128)S(1)}) custom-call(f32[4,512,256]{2,1,0:T(8,128)S(1)} %bitcast.32, f32[1,256]{1,0:T(1,128)S(1)} %copy-done), custom_call_target="tpu_custom_call" | custom-call | tf_op jit(solution)/shard_map/key_reduce/pallas_call | solution.py:219
  214.5 27.2 %value_scale.1 = f32[32768,256]{1,0:T(8,128)} custom-call(f32[1]{0:T(128)} %bitcast.11.factor_ref, f32[32768,256]{1,0:T(8,128)} %get-tuple-element.9.grad_ref), custom_call_target="tpu_custom_call" | custom-call | tf_op jit(solution)/shard_map/value_scale/pallas_call | solution.py:395
  (79 shorter events, 10.7 us)
Async XLA Ops:
  7.2 17.7 %copy-start.1 = (bf16[2,2,512,256]{3,2,1,0:T(8,128)(2,1)S(1)}, bf16[2,2,512,256]{3,2,1,0:T(8,128)(2,1)}, u32[]{:S(2)}) copy-start(bf16[2,2,512,256]{3,2,1,0:T(8,128)(2,1)} %param.7) | copy-start | bytes 3145732
  8.9 15.2 %all-to-all-start.1 = ((bf16[128,4,256]{2,0,1:T(8,128)(2,1)}), bf16[128,4,256]{2,0,1:T(8,128)(2,1)S(1)}, u32[]{:S(2)}, u32[]{:S(2)}) async-start(bf16[128,4,256]{2,0,1:T(8,128)(2,1)} %bitcast.31), calls=%async_computation.1 | async-start | bytes 524288 | tf_op jit(solution)/shard_map/all_to_all | solution.py:275
  15.3 37.5 %all-gather.2.cloned.1.call-start = ((), (), s32[]{:S(2)}) async-start(), calls=%async_computation.3 | async-start | bytes 2359296 | tf_op jit(solution)/shard_map/all_gather | solution.py:276
  24.2 0.7 copy-start.2
  24.9 1.0 copy-start.3
  24.9 1.0 copy-start.4
  30.4 11.3 %all-to-all-start = ((f32[32,1,576]{2,1,0:T(1,128)}), f32[32,1,576]{2,1,0:T(1,128)S(1)}, u32[]{:S(2)}, u32[]{:S(2)}) async-start(f32[32,1,576]{2,1,0:T(1,128)} %all_to_all.26), calls=%async_computation | async-start | bytes 163840 | tf_op jit(solution)/shard_map/all_to_all | solution.py:317
  101.8 68.8 %all-to-all-start.2 = ((f32[32,1,192]{2,1,0:T(1,128)}), f32[32,1,192]{2,1,0:T(1,128)S(1)}, u32[]{:S(2)}, u32[]{:S(2)}) async-start(f32[32,1,192]{2,1,0:T(1,128)} %all_to_all.34), calls=%async_computation.2 | async-start | bytes 65536 | tf_op jit(solution)/shard_map/all_to_all | solution.py:348
  174.4 0.6 copy-start
Sparse Core Ops, SparseCore 0:
  25.0 27.6 all-gather.1
